TPU v7x, 32 devices: a whole 2x2x4 slice. The times are simulated.
32 devices in a mesh: groups: 2 (over x), blk: 16 (over z, y, core).
Axes of the slice: x: 2, y: 2, z: 4, core: 2. Of those that a mesh axis runs over, the one named last changes fastest.
Arguments:
- train_acts: bfloat16 [4096, 768], P(('groups', 'blk')), parts along dimension 0, may hold values from -6 to 6
- train_grads: bfloat16 [4096, 2048], P(('groups', 'blk')), parts along dimension 0, may hold values from -0.059814453 to 0.059814453
- train_expert: int32 [4096, 1], P(('groups', 'blk')), parts along dimension 0, may hold values from 0 to 1; in each aligned block of 128 rows (0 to 127, 128 to 255, ...) at most 96 rows name the same one
- train_doc: int32 [4096], P(('groups', 'blk')), parts along dimension 0, may hold values from 0 to 3
- query_acts: bfloat16 [64, 768], P('blk'), may hold values from -6 to 6
- query_grads: bfloat16 [64, 2048], P('blk'), may hold values from -0.059814453 to 0.059814453
- query_expert: int32 [64, 1], P('blk'), may hold values from 0 to 1; in each aligned block of 4 rows (0 to 3, 4 to 7, ...) at most 3 rows name the same one
- query_ids: int32 [64], P('blk'), may hold values from 0 to 1
- basis_out: bfloat16 [2, 2048, 2048], P(None, None, 'blk'), may hold values from -0.125 to 0.125
- basis_in: bfloat16 [2, 768, 768], P(None, None, 'blk'), may hold values from -0.21875 to 0.21875
- eigenvalues: bfloat16 [2, 2048, 768], P(None, 'blk'), may hold values from 0.019897461 to 5
Outputs:
- scores: float32 [128, 32], P(('groups', 'blk')), parts along dimension 0
There are 2 independent parts, one for each index of `groups`. A program takes and returns all parts, laid end to end along the dimension named above; an argument that names none is the same for every part. Nothing has to cross between parts.
Inputs may be any that keep to these rules, and one draw needn't show every extreme that they name: `train_expert`: the rows of one device name each expert at most 96 times; in every draw some device's rows name one expert exactly 96 times. `query_expert`: the rows of one device name each expert at most 3 times; in every draw some device's rows name one expert exactly 3 times.
All inputs are finite; a program needn't handle non-finite values.
Results may differ from a plain program's by a relative error of at most 0.0053.
Values may be sent and summed in bfloat16 or wider, within the bound.
A program may use at most 128 MiB of HBM per device.

v0:
```python
import jax
import jax.numpy as jnp
from jax import lax
from jax.sharding import PartitionSpec as P

DOCS_DEV = 4
QRY_DEV = 2
CAP = 96
QCAP = 3
DAMPING = 0.05


def slot_table(experts, capacity, count):
    rows = experts.shape[0]
    onehot = (experts[:, None] == jnp.arange(count, dtype=jnp.int32)[None, :]).astype(jnp.int32)
    before = jnp.cumsum(onehot, axis=0) - onehot
    rank = jnp.sum(before * onehot, axis=1)
    target = experts * capacity + rank
    source = (
        jnp.zeros((count * capacity,), jnp.int32).at[target].set(jnp.arange(rows, dtype=jnp.int32))
    )
    filled = jnp.zeros((count * capacity,), jnp.int32).at[target].set(1)
    return (source.reshape(count, capacity), filled.reshape(count, capacity))


def turner(rows, piece):
    return jnp.einsum("ecd,edn->ecn", rows, piece, preferred_element_type=jnp.float32)


def body(
    train_acts,
    train_grads,
    train_expert,
    train_doc,
    query_acts,
    query_grads,
    query_expert,
    query_ids,
    basis_out,
    basis_in,
    eigenvalues,
):
    count = basis_out.shape[0]
    train_src, train_fill = slot_table(train_expert[:, 0], CAP, count)
    query_src, query_fill = slot_table(query_expert[:, 0], QCAP, count)
    source = jnp.concatenate([train_src, query_src + train_acts.shape[0]], axis=1)
    filled = jnp.concatenate([train_fill, query_fill], axis=1)
    weight = filled.astype(jnp.bfloat16)[:, :, None]
    grads_in = jnp.concatenate([train_grads, query_grads], axis=0)[source] * weight
    acts_in = jnp.concatenate([train_acts, query_acts], axis=0)[source] * weight
    slot_doc = train_doc[train_src]
    queries_total = QRY_DEV * lax.axis_size("blk")
    global_ids = jnp.where(
        query_fill == 1, lax.axis_index("blk") * QRY_DEV + query_ids[query_src], -1
    )
    rot_grads = turner(grads_in, lax.all_gather(basis_out, "blk", axis=2, tiled=True))
    rot_acts = turner(acts_in, lax.all_gather(basis_in, "blk", axis=2, tiled=True))
    rot_grads = rot_grads.astype(jnp.bfloat16)
    rot_acts = rot_acts.astype(jnp.bfloat16)
    train_g = rot_grads[:, :CAP]
    train_a = rot_acts[:, :CAP]
    query_g = rot_grads[:, CAP:]
    query_a = rot_acts[:, CAP:]
    doc_masks = [
        ((slot_doc == doc) & (train_fill == 1)).astype(jnp.bfloat16) for doc in range(DOCS_DEV)
    ]
    scale = lax.all_gather(eigenvalues, "blk", axis=1, tiled=True).astype(jnp.float32) + DAMPING
    mats = []
    for mask in doc_masks:
        summed = jnp.einsum(
            "ecn,ecf->enf", train_g * mask[:, :, None], train_a, preferred_element_type=jnp.float32
        )
        mats.append((summed / scale).astype(jnp.bfloat16))
    doc_mats = jnp.stack(mats)
    piece_g, piece_a, piece_ids = lax.all_gather(
        (query_g, query_a, global_ids), "blk", axis=1, tiled=True
    )
    image = jnp.einsum("esf,kedf->kesd", piece_a, doc_mats, preferred_element_type=jnp.float32)
    token = jnp.einsum("kesd,esd->esk", image, piece_g.astype(jnp.float32))
    table = (
        piece_ids.reshape(-1)[:, None] == jnp.arange(queries_total, dtype=jnp.int32)[None, :]
    ).astype(jnp.float32)
    return jnp.dot(token.reshape(-1, DOCS_DEV).T, table, precision=lax.Precision.HIGHEST)


def solution(mesh):
    in_specs = (
        P(("groups", "blk"), None),
        P(("groups", "blk"), None),
        P(("groups", "blk"), None),
        P(("groups", "blk")),
        P("blk", None),
        P("blk", None),
        P("blk", None),
        P("blk"),
        P(None, None, "blk"),
        P(None, None, "blk"),
        P(None, "blk", None),
    )
    out_specs = P(("groups", "blk"), None)
    return jax.shard_map(body, mesh=mesh, in_specs=in_specs, out_specs=out_specs, check_vma=False)
```

profile of v0, /device:TPU:0, one launch (start us, length us, event | category | flops | bytes accessed | tf_op | source)
XLA Modules:
  0.0 286.9 jit_solution(85553088531195338)
XLA Ops:
  12.3 1.3 gather_fusion.3
  13.7 0.7 fusion.33
  14.6 0.8 select_reduce_fusion
  16.1 1.0 scatter_custom_fusion.2
  17.2 1.0 scatter_custom_fusion
  18.5 1.1 pad_maximum_fusion.1
  19.7 1.2 gather_fusion
  21.1 1.0 gather_fusion.2
  22.3 1.6 gather_fusion.1
  24.3 23.1 %all-gather = s32[16,3,2]{1,2,0:T(2,128)S(1)} all-gather(s32[1,3,2]{1,2,0:T(2,128)S(1)} %bitcast.49), channel_id=1, replica_groups=mesh['groups'=2,'blk'=16] {'blk'}, dimensions={0}, use_global_device_ids=true | all-gather | bytes 408 | tf_op jit(solution)/shard_map/all_gather | solution.py:75
  47.6 7.1 %all-gather.7.cloned.1.call-done = bf16[2,768,768]{1,2,0:T(8,128)(2,1)} async-done(((bf16[2,768,48]{1,2,0:T(8,128)(2,1)}), bf16[2,768,768]{1,2,0:T(8,128)(2,1)}) %all-gather.7.cloned.1.call-update) | async-done | bytes 2359312 | tf_op jit(solution)/shard_map/all_gather | solution.py:57
  54.8 2.5 convolution_convert_fusion.1
  57.3 20.2 %all_gather.21 = bf16[2,48,768]{2,0,1:T(2,128)(2,1)S(1)} all-gather(bf16[2,3,768]{2,0,1:T(2,128)(2,1)S(1)} %copy.20), channel_id=1, replica_groups=mesh['groups'=2,'blk'=16] {'blk'}, dimensions={1}, use_global_device_ids=true | all-gather | bytes 156672 | tf_op jit(solution)/shard_map/all_gather | solution.py:75
  77.5 109.2 %all-gather.5.cloned.1.call-done = bf16[2,2048,2048]{2,1,0:T(8,128)(2,1)} async-done(((bf16[2,2048,128]{2,1,0:T(8,128)(2,1)}), bf16[2,2048,2048]{2,1,0:T(8,128)(2,1)}) %all-gather.5.cloned.1.call-update) | async-done | bytes 16777232 | tf_op jit(solution)/shard_map/all_gather | solution.py:56
  186.7 8.5 %convolution_convert_fusion = bf16[2,99,2048]{2,1,0:T(8,128)(2,1)S(1)} fusion(bf16[2,2048,2048]{2,1,0:T(8,128)(2,1)} %all-gather.5.cloned.1.call-done, bf16[2,99,2048]{2,1,0:T(8,128)(2,1)S(1)} %reshape.209, bf16[2,99]{1,0:T(2,128)(2,1)S(1)} %pad_maximum_fusion.3), kind=kOutput, calls=%fused_computation.23 | convolution fusion | flops 1661755392 | bytes 18399628 | tf_op jit(solution)/shard_map/ecd,edn->ecn/dot_general | solution.py:27
  195.2 22.0 %all_gather.22 = bf16[2,48,2048]{2,0,1:T(2,128)(2,1)S(1)} all-gather(bf16[2,3,2048]{2,0,1:T(2,128)(2,1)S(1)} %copy.23), channel_id=1, replica_groups=mesh['groups'=2,'blk'=16] {'blk'}, dimensions={1}, use_global_device_ids=true | all-gather | bytes 417792 | tf_op jit(solution)/shard_map/all_gather | solution.py:75
  217.2 33.7 %all-gather.9.cloned.1.call-done = bf16[2,2048,768]{2,1,0:T(8,128)(2,1)} async-done(((bf16[2,128,768]{2,1,0:T(8,128)(2,1)}), bf16[2,2048,768]{2,1,0:T(8,128)(2,1)}) %all-gather.9.cloned.1.call-update) | async-done | bytes 6291472 | tf_op jit(solution)/shard_map/all_gather | solution.py:67
  250.9 4.9 %fusion.3 = bf16[1,2,2048,768]{3,2,1,0:T(8,128)(2,1)S(1)} fusion(bf16[2,2048,768]{2,1,0:T(8,128)(2,1)} %all-gather.9.cloned.1.call-done, bf16[2,99,2048]{2,1,0:T(8,128)(2,1)S(1)} %convolution_convert_fusion, bf16[2,96]{1,0:T(2,128)(2,1)S(1)} %reshape.293, bf16[2,99,768]{2,1,0:T(8,128)(2,1)S(1)} %convolution_convert_fusion.1), kind=kOutput, calls=%fused_computation.17 | convolution fusion | flops 616955904 | bytes 13664768 | tf_op jit(solution)/shard_map/ecn,ecf->enf/dot_general | solution.py:70
  255.8 2.5 fusion.4
  258.3 4.2 %fusion.5 = bf16[1,2,2048,768]{3,2,1,0:T(8,128)(2,1)} fusion(bf16[2,2048,768]{2,1,0:T(8,128)(2,1)S(1)} %copy-done.3, bf16[2,99,2048]{2,1,0:T(8,128)(2,1)S(1)} %convolution_convert_fusion, bf16[2,96]{1,0:T(2,128)(2,1)S(1)} %reshape.295, bf16[2,99,768]{2,1,0:T(8,128)(2,1)S(1)} %convolution_convert_fusion.1), kind=kOutput, calls=%fused_computation.19 | convolution fusion | flops 616955904 | bytes 13664768 | tf_op jit(solution)/shard_map/ecn,ecf->enf/dot_general | solution.py:70
  262.4 4.1 %fusion.2 = bf16[1,2,2048,768]{3,2,1,0:T(8,128)(2,1)} fusion(bf16[2,2048,768]{2,1,0:T(8,128)(2,1)S(1)} %copy-done.3, bf16[2,99,2048]{2,1,0:T(8,128)(2,1)S(1)} %convolution_convert_fusion, bf16[2,96]{1,0:T(2,128)(2,1)S(1)} %reshape.292, bf16[2,99,768]{2,1,0:T(8,128)(2,1)S(1)} %convolution_convert_fusion.1), kind=kOutput, calls=%fused_computation.16 | convolution fusion | flops 616955904 | bytes 13664768 | tf_op jit(solution)/shard_map/ecn,ecf->enf/dot_general | solution.py:70
  266.5 10.9 %fusion.8 = bf16[4,2,48,2048]{3,2,0,1:T(8,128)(2,1)S(1)} fusion(bf16[2,48,768,1]{2,0,1,3:T(2,128)(2,1)S(1)} %bitcast.46, bf16[1,2,2048,768]{3,2,1,0:T(8,128)(2,1)} %fusion.5, bf16[1,2,2048,768]{3,2,1,0:T(8,128)(2,1)S(1)} %fusion.4, bf16[1,2,2048,768]{3,2,1,0:T(8,128)(2,1)S(1)} %fusion.3, bf16[1,2,2048,768]{3,2,1,0:T(8,128)(2,1)} %fusion.2), kind=kOutput, calls=%fused_computation.22 | convolution fusion | flops 1245708288 | bytes 26886144 | tf_op jit(solution)/shard_map/esf,kedf->kesd/dot_general | solution.py:78
  277.4 2.2 fusion.6
  279.6 0.8 fusion.34
  (61 shorter events, 8.2 us)
Async XLA Ops:
  6.5 15.7 %copy-start = (s32[128]{0:T(128)S(1)}, s32[128]{0:T(128)}, u32[]{:S(2)}) copy-start(s32[128]{0:T(128)} %param.14) | copy-start | bytes 1540
  6.5 48.2 %all-gather.7.cloned.1.call-start = ((), (), s32[]{:S(2)}) async-start(), calls=%async_computation.1 | async-start | bytes 2506752 | tf_op jit(solution)/shard_map/all_gather | solution.py:57
  7.3 179.4 %all-gather.5.cloned.1.call-start = ((), (), s32[]{:S(2)}) async-start(), calls=%async_computation | async-start | bytes 17825792 | tf_op jit(solution)/shard_map/all_gather | solution.py:56
  8.0 13.0 %copy-start.1 = (bf16[128,768]{1,0:T(8,128)(2,1)S(1)}, bf16[128,768]{1,0:T(8,128)(2,1)}, u32[]{:S(2)}) copy-start(bf16[128,768]{1,0:T(8,128)(2,1)} %param.11) | copy-start | bytes 589828
  8.0 13.0 %copy-start.2 = (bf16[4,768]{1,0:T(4,128)(2,1)S(1)}, bf16[4,768]{1,0:T(4,128)(2,1)}, u32[]{:S(2)}) copy-start(bf16[4,768]{1,0:T(4,128)(2,1)} %param.15) | copy-start | bytes 18436
  8.0 242.9 %all-gather.9.cloned.1.call-start = ((), (), s32[]{:S(2)}) async-start(), calls=%async_computation.2 | async-start | bytes 6684672 | tf_op jit(solution)/shard_map/all_gather | solution.py:67
  250.9 4.9 %copy-start.3 = (bf16[2,2048,768]{2,1,0:T(8,128)(2,1)S(1)}, bf16[2,2048,768]{2,1,0:T(8,128)(2,1)}, u32[]{:S(2)}) copy-start(bf16[2,2048,768]{2,1,0:T(8,128)(2,1)} %all-gather.9.cloned.1.call-done) | copy-start | bytes 18874372
Sparse Core Ops, SparseCore 0:
  9.6 45.0 all-gather.6
  56.9 129.7 all-gather.4
  189.0 61.8 all-gather.8
where the time goes:
time: 287 us
  waiting for transfers between devices  152 us (53%)
  blocking collectives  65.3 us (23%)
  matrix products  40.5 us (14%)
  between operations  13.4 us (5%)
  local copies, waits for them, and re-layouts  9.76 us (3%)
  other arithmetic  5.92 us (2%)
    all_gather x1, waiting for transfers between devices, body(): lax.all_gather(basis_out, 'blk', axis=2, tiled=True)  109 us
    all_gather x3, blocking collectives, body(): lax.all_gather((query_g, query_a, global_ids), 'blk', axis=1, tiled=True)  65.3 us
    all_gather x1, waiting for transfers between devices, body(): lax.all_gather(eigenvalues, 'blk', axis=1, tiled=True).astype(jnp.float32)  33.7 us
    dot_general x4, matrix products, body(): jnp.einsum('ecn,ecf->enf', train_g * mask[:, :, None], train_a, preferred...  15.6 us
    dot_general x2, matrix products, turner(): jnp.einsum('ecd,edn->ecn', rows, piece, preferred_element_type=jnp.float32)  11 us
    dot_general x1, matrix products, body(): jnp.einsum('esf,kedf->kesd', piece_a, doc_mats, preferred_element_type=jn...  10.9 us
    all_gather x1, waiting for transfers between devices, body(): lax.all_gather(basis_in, 'blk', axis=2, tiled=True)  7.12 us
  transfers between devices with their start and end apart: 3, of which 3 were waited for; matrix products, arithmetic and copies ran while one was open for 9% of the time, Pallas kernels for 0%

commit v1 on v0

--- a/solution.py
+++ b/solution.py
@@ -8,6 +8,27 @@
 CAP = 96
 QCAP = 3
 DAMPING = 0.05
+
+
+def launch_body(inp):
+    placed, right_arr, wide_out = (lax.psum(1, "blk"), lax.axis_index("blk"), inp.shape[1])
+    all_blocks = tuple(((kk, (kk + 1) % placed) for kk in range(placed)))
+    column = tuple(((kk, (kk - 1) % placed) for kk in range(placed)))
+    mat_out = jnp.zeros((*inp.shape[:1], placed * wide_out, *inp.shape[2:]), inp.dtype)
+    mat_out = lax.dynamic_update_slice_in_dim(mat_out, inp, right_arr * wide_out, axis=1)
+    y_new = tmp = inp
+    m_next = placed // 2
+    for t in range(1, m_next + 1):
+        y_new = lax.ppermute(y_new, "blk", all_blocks)
+        mat_out = lax.dynamic_update_slice_in_dim(
+            mat_out, y_new, (right_arr - t) % placed * wide_out, axis=1
+        )
+        if t < placed - m_next:
+            tmp = lax.ppermute(tmp, "blk", column)
+            mat_out = lax.dynamic_update_slice_in_dim(
+                mat_out, tmp, (right_arr + t) % placed * wide_out, axis=1
+            )
+    return mat_out
 
 
 def slot_table(experts, capacity, count):
@@ -64,7 +85,7 @@
     doc_masks = [
         ((slot_doc == doc) & (train_fill == 1)).astype(jnp.bfloat16) for doc in range(DOCS_DEV)
     ]
-    scale = lax.all_gather(eigenvalues, "blk", axis=1, tiled=True).astype(jnp.float32) + DAMPING
+    scale = launch_body(eigenvalues).astype(jnp.float32) + DAMPING
     mats = []
     for mask in doc_masks:
         summed = jnp.einsum(

time: 287 us -> 275 us (0.958)
  waiting for transfers between devices: 152 us -> 92.9 us
  starting transfers between devices: 0.08 us -> 29.5 us
  local copies, waits for them, and re-layouts: 9.76 us -> 29.5 us
  blocking collectives: 65.3 us -> 62.4 us
    all_gather x1, waiting for transfers between devices: 109 us -> 38.2 us  [body(): lax.all_gather(basis_out, 'blk', axis=2, tiled=True)]
    ppermute x0 -> x15, waiting for transfers between devices: none -> 53.3 us  [the longest x8 28.7 us: launch_body(): y_new = lax.ppermute(y_new, 'blk', all_blocks)]
    all_gather x1 -> x0, waiting for transfers between devices: 33.7 us -> none  [body(): lax.all_gather(eigenvalues, 'blk', axis=1, tiled=True).astype(jnp.float32)]
    ppermute x0 -> x15, starting transfers between devices: none -> 29.4 us  [the longest x7 28.9 us: launch_body(): tmp = lax.ppermute(tmp, 'blk', column)]
    dynamic_update_slice x0 -> x16, local copies, waits for them, and re-layouts: none -> 16.7 us  [the longest x8 8.36 us: launch_body(): lax.dynamic_update_slice_in_dim(mat_out, y_new, (right_arr - t) % placed...]
    all_gather x1, waiting for transfers between devices: 7.12 us -> 0.01 us  [body(): lax.all_gather(basis_in, 'blk', axis=2, tiled=True)]
    broadcast_in_dim x0 -> x1, local copies, waits for them, and re-layouts: none -> 3.06 us  [launch_body(): jnp.zeros((*inp.shape[:1], placed * wide_out, *inp.shape[2:]), inp.dtype)]
  transfers between devices with their start and end apart: 3 -> 17, of which waited for: 3 -> 8; matrix products, arithmetic and copies ran while one was open for 9% -> 14% of each run, Pallas kernels for 0% -> 0%
where the time goes in v1:
time: 275 us
  waiting for transfers between devices  92.9 us (34%)
  blocking collectives  62.4 us (23%)
  matrix products  39.6 us (14%)
  local copies, waits for them, and re-layouts  29.5 us (11%)
  starting transfers between devices  29.5 us (11%)
  between operations  14 us (5%)
  other arithmetic  6.85 us (2%)
    all_gather x3, blocking collectives, body(): lax.all_gather((query_g, query_a, global_ids), 'blk', axis=1, tiled=True)  62.4 us
    all_gather x1, waiting for transfers between devices, body(): lax.all_gather(basis_out, 'blk', axis=2, tiled=True)  38.2 us
    ppermute x7, starting transfers between devices, launch_body(): tmp = lax.ppermute(tmp, 'blk', column)  28.9 us
    ppermute x8, waiting for transfers between devices, launch_body(): y_new = lax.ppermute(y_new, 'blk', all_blocks)  28.7 us
    ppermute x7, waiting for transfers between devices, launch_body(): tmp = lax.ppermute(tmp, 'blk', column)  24.6 us
    dot_general x4, matrix products, body(): jnp.einsum('ecn,ecf->enf', train_g * mask[:, :, None], train_a, preferred...  17.3 us
    dot_general x2, matrix products, turner(): jnp.einsum('ecd,edn->ecn', rows, piece, preferred_element_type=jnp.float32)  11 us
    dynamic_update_slice x8, local copies, waits for them, and re-layouts, launch_body(): lax.dynamic_update_slice_in_dim(mat_out, y_new, (right_arr - t) % placed...  8.36 us
  transfers between devices with their start and end apart: 17, of which 8 were waited for; matrix products, arithmetic and copies ran while one was open for 14% of the time, Pallas kernels for 0%

profile of v1, /device:TPU:0, one launch (start us, length us, event | category | flops | bytes accessed | tf_op | source)
XLA Modules:
  0.0 274.8 jit_solution(12730324649266534088)
XLA Ops:
  8.5 5.1 %collective-permute-start.1 = (bf16[2,128,768]{2,1,0:T(8,128)(2,1)}, bf16[2,128,768]{2,1,0:T(8,128)(2,1)S(1)}, u32[]{:S(2)}, u32[]{:S(2)}) collective-permute-start(bf16[2,128,768]{2,1,0:T(8,128)(2,1)} %param.21), channel_id=1, source_target_pairs={{0,15},{1,0},{2,1},{3,2},{4,3},{5,4},{6,5},{7,6},{8,7},{9,8},{10,9... | collective-permute-start | bytes 1179656 | tf_op jit(solution)/shard_map/ppermute | solution.py:27
  24.7 4.5 %collective-permute-start.3 = (bf16[2,128,768]{2,1,0:T(8,128)(2,1)S(1)}, bf16[2,128,768]{2,1,0:T(8,128)(2,1)S(1)}, u32[]{:S(2)}, u32[]{:S(2)}) collective-permute-start(bf16[2,128,768]{2,1,0:T(8,128)(2,1)S(1)} %collective-permute-done.1), channel_id=1, source_target_pairs={{0,15},{1,0},{2,1},{3,2},{4,3},{5,4},{6,5},{7,6},{8,7},{9,8},{10,9... | collective-permute-start | bytes 1179656 | tf_op jit(solution)/shard_map/ppermute | solution.py:27
  29.2 6.9 %collective-permute-done.2 = bf16[2,128,768]{2,1,0:T(8,128)(2,1)S(1)} collective-permute-done((bf16[2,128,768]{2,1,0:T(8,128)(2,1)S(1)}, bf16[2,128,768]{2,1,0:T(8,128)(2,1)S(1)}, u32[]{:S(2)}, u32[]{:S(2)}) %collective-permute-start.2) | collective-permute-done | bytes 393248 | tf_op jit(solution)/shard_map/ppermute | solution.py:22
  36.1 4.5 %collective-permute-start.5 = (bf16[2,128,768]{2,1,0:T(8,128)(2,1)S(1)}, bf16[2,128,768]{2,1,0:T(8,128)(2,1)}, u32[]{:S(2)}, u32[]{:S(2)}) collective-permute-start(bf16[2,128,768]{2,1,0:T(8,128)(2,1)S(1)} %collective-permute-done.3), channel_id=1, source_target_pairs={{0,15},{1,0},{2,1},{3,2},{4,3},{5,4},{6,5},{7,6},{8,7},{9,8},{10,9... | collective-permute-start | bytes 1179656 | tf_op jit(solution)/shard_map/ppermute | solution.py:27
  41.6 9.9 %collective-permute-done.4 = bf16[2,128,768]{2,1,0:T(8,128)(2,1)S(1)} collective-permute-done((bf16[2,128,768]{2,1,0:T(8,128)(2,1)S(1)}, bf16[2,128,768]{2,1,0:T(8,128)(2,1)S(1)}, u32[]{:S(2)}, u32[]{:S(2)}) %collective-permute-start.4) | collective-permute-done | bytes 393248 | tf_op jit(solution)/shard_map/ppermute | solution.py:22
  52.8 4.5 %collective-permute-start.7 = (bf16[2,128,768]{2,1,0:T(8,128)(2,1)}, bf16[2,128,768]{2,1,0:T(8,128)(2,1)}, u32[]{:S(2)}, u32[]{:S(2)}) collective-permute-start(bf16[2,128,768]{2,1,0:T(8,128)(2,1)} %collective-permute-done.5), channel_id=1, source_target_pairs={{0,15},{1,0},{2,1},{3,2},{4,3},{5,4},{6,5},{7,6},{8,7},{9,8},{10,9... | collective-permute-start | bytes 1179656 | tf_op jit(solution)/shard_map/ppermute | solution.py:27
  57.5 7.2 %collective-permute-done.6 = bf16[2,128,768]{2,1,0:T(8,128)(2,1)} collective-permute-done((bf16[2,128,768]{2,1,0:T(8,128)(2,1)S(1)}, bf16[2,128,768]{2,1,0:T(8,128)(2,1)}, u32[]{:S(2)}, u32[]{:S(2)}) %collective-permute-start.6) | collective-permute-done | bytes 393248 | tf_op jit(solution)/shard_map/ppermute | solution.py:22
  67.9 18.0 %all-gather = s32[16,3,2]{1,2,0:T(2,128)S(1)} all-gather(s32[1,3,2]{1,2,0:T(2,128)S(1)} %bitcast.49), channel_id=1, replica_groups=mesh['groups'=2,'blk'=16] {'blk'}, dimensions={0}, use_global_device_ids=true | all-gather | bytes 408 | tf_op jit(solution)/shard_map/all_gather | solution.py:96
  86.1 3.1 %broadcast_in_dim.8 = bf16[2,2048,768]{2,1,0:T(8,128)(2,1)} broadcast(bf16[]{:T(256)} %constant.128.clone.1), dimensions={} | broadcast | bytes 6291458 | tf_op jit(solution)/shard_map/broadcast_in_dim | solution.py:17
  95.1 10.8 %collective-permute-done.9 = bf16[2,128,768]{2,1,0:T(8,128)(2,1)S(1)} collective-permute-done((bf16[2,128,768]{2,1,0:T(8,128)(2,1)}, bf16[2,128,768]{2,1,0:T(8,128)(2,1)S(1)}, u32[]{:S(2)}, u32[]{:S(2)}) %collective-permute-start.9) | collective-permute-done | bytes 393248 | tf_op jit(solution)/shard_map/ppermute | solution.py:27
  105.9 4.5 %collective-permute-start.11 = (bf16[2,128,768]{2,1,0:T(8,128)(2,1)S(1)}, bf16[2,128,768]{2,1,0:T(8,128)(2,1)S(1)}, u32[]{:S(2)}, u32[]{:S(2)}) collective-permute-start(bf16[2,128,768]{2,1,0:T(8,128)(2,1)S(1)} %collective-permute-done.9), channel_id=1, source_target_pairs={{0,15},{1,0},{2,1},{3,2},{4,3},{5,4},{6,5},{7,6},{8,7},{9,8},{10,9... | collective-permute-start | bytes 1179656 | tf_op jit(solution)/shard_map/ppermute | solution.py:27
  117.6 3.6 %collective-permute-done.11 = bf16[2,128,768]{2,1,0:T(8,128)(2,1)S(1)} collective-permute-done((bf16[2,128,768]{2,1,0:T(8,128)(2,1)S(1)}, bf16[2,128,768]{2,1,0:T(8,128)(2,1)S(1)}, u32[]{:S(2)}, u32[]{:S(2)}) %collective-permute-start.11) | collective-permute-done | bytes 393248 | tf_op jit(solution)/shard_map/ppermute | solution.py:27
  121.2 4.7 %collective-permute-start.13 = (bf16[2,128,768]{2,1,0:T(8,128)(2,1)S(1)}, bf16[2,128,768]{2,1,0:T(8,128)(2,1)S(1)}, u32[]{:S(2)}, u32[]{:S(2)}) collective-permute-start(bf16[2,128,768]{2,1,0:T(8,128)(2,1)S(1)} %collective-permute-done.11), channel_id=1, source_target_pairs={{0,15},{1,0},{2,1},{3,2},{4,3},{5,4},{6,5},{7,6},{8,7},{9,8},{10,9... | collective-permute-start | bytes 1179656 | tf_op jit(solution)/shard_map/ppermute | solution.py:27
  129.1 10.2 %collective-permute-done.13 = bf16[2,128,768]{2,1,0:T(8,128)(2,1)S(1)} collective-permute-done((bf16[2,128,768]{2,1,0:T(8,128)(2,1)S(1)}, bf16[2,128,768]{2,1,0:T(8,128)(2,1)S(1)}, u32[]{:S(2)}, u32[]{:S(2)}) %collective-permute-start.13) | collective-permute-done | bytes 393248 | tf_op jit(solution)/shard_map/ppermute | solution.py:27
  140.1 4.7 %collective-permute-done.14 = bf16[2,128,768]{2,1,0:T(8,128)(2,1)S(1)} collective-permute-done((bf16[2,128,768]{2,1,0:T(8,128)(2,1)S(1)}, bf16[2,128,768]{2,1,0:T(8,128)(2,1)S(1)}, u32[]{:S(2)}, u32[]{:S(2)}) %collective-permute-start.14) | collective-permute-done | bytes 393248 | tf_op jit(solution)/shard_map/ppermute | solution.py:22
  148.2 23.5 %all_gather.17 = bf16[2,48,768]{2,0,1:T(2,128)(2,1)S(1)} all-gather(bf16[2,3,768]{2,0,1:T(2,128)(2,1)S(1)} %copy.20), channel_id=1, replica_groups=mesh['groups'=2,'blk'=16] {'blk'}, dimensions={1}, use_global_device_ids=true | all-gather | bytes 156672 | tf_op jit(solution)/shard_map/all_gather | solution.py:96
  171.7 38.2 %all-gather.4.cloned.1.call-done = bf16[2,2048,2048]{2,1,0:T(8,128)(2,1)} async-done(((bf16[2,2048,128]{2,1,0:T(8,128)(2,1)}), bf16[2,2048,2048]{2,1,0:T(8,128)(2,1)}) %all-gather.4.cloned.1.call-update) | async-done | bytes 16777232 | tf_op jit(solution)/shard_map/all_gather | solution.py:77
  209.9 8.5 %convolution_convert_fusion = bf16[2,99,2048]{2,1,0:T(8,128)(2,1)S(1)} fusion(bf16[2,2048,2048]{2,1,0:T(8,128)(2,1)} %all-gather.4.cloned.1.call-done, bf16[2,99,2048]{2,1,0:T(8,128)(2,1)S(1)} %reshape.209, bf16[2,99]{1,0:T(2,128)(2,1)S(1)} %pad_maximum_fusion.3), kind=kOutput, calls=%fused_computation.23 | convolution fusion | flops 1661755392 | bytes 18399628 | tf_op jit(solution)/shard_map/ecd,edn->ecn/dot_general | solution.py:48
  218.4 4.3 %fusion.3 = bf16[1,2,2048,768]{3,2,1,0:T(8,128)(2,1)S(1)} fusion(bf16[2,2048,768]{2,1,0:T(8,128)(2,1)} %constant_dynamic-update-slice_fusion, bf16[2,99,2048]{2,1,0:T(8,128)(2,1)S(1)} %convolution_convert_fusion, bf16[2,96]{1,0:T(2,128)(2,1)S(1)} %reshape.293, bf16[2,99,768]{2,1,0:T(8,128)(2,1)S(1)} %convolution_convert_fusion.1), kind=kOutput, calls=%fused_computation.17 | convolution fusion | flops 616955904 | bytes 13664768 | tf_op jit(solution)/shard_map/ecn,ecf->enf/dot_general | solution.py:91
  222.7 4.3 %fusion.4 = bf16[1,2,2048,768]{3,2,1,0:T(8,128)(2,1)S(1)} fusion(bf16[2,2048,768]{2,1,0:T(8,128)(2,1)} %constant_dynamic-update-slice_fusion, bf16[2,99,2048]{2,1,0:T(8,128)(2,1)S(1)} %convolution_convert_fusion, bf16[2,96]{1,0:T(2,128)(2,1)S(1)} %reshape.294, bf16[2,99,768]{2,1,0:T(8,128)(2,1)S(1)} %convolution_convert_fusion.1), kind=kOutput, calls=%fused_computation.18 | convolution fusion | flops 616955904 | bytes 13664768 | tf_op jit(solution)/shard_map/ecn,ecf->enf/dot_general | solution.py:91
  227.0 4.3 %fusion.2 = bf16[1,2,2048,768]{3,2,1,0:T(8,128)(2,1)S(1)} fusion(bf16[2,2048,768]{2,1,0:T(8,128)(2,1)} %constant_dynamic-update-slice_fusion, bf16[2,99,2048]{2,1,0:T(8,128)(2,1)S(1)} %convolution_convert_fusion, bf16[2,96]{1,0:T(2,128)(2,1)S(1)} %reshape.292, bf16[2,99,768]{2,1,0:T(8,128)(2,1)S(1)} %convolution_convert_fusion.1), kind=kOutput, calls=%fused_computation.16 | convolution fusion | flops 616955904 | bytes 13664768 | tf_op jit(solution)/shard_map/ecn,ecf->enf/dot_general | solution.py:91
  231.3 4.3 %fusion.5 = bf16[1,2,2048,768]{3,2,1,0:T(8,128)(2,1)S(1)} fusion(bf16[2,2048,768]{2,1,0:T(8,128)(2,1)} %constant_dynamic-update-slice_fusion, bf16[2,99,2048]{2,1,0:T(8,128)(2,1)S(1)} %convolution_convert_fusion, bf16[2,96]{1,0:T(2,128)(2,1)S(1)} %reshape.295, bf16[2,99,768]{2,1,0:T(8,128)(2,1)S(1)} %convolution_convert_fusion.1), kind=kOutput, calls=%fused_computation.19 | convolution fusion | flops 616955904 | bytes 13664768 | tf_op jit(solution)/shard_map/ecn,ecf->enf/dot_general | solution.py:91
  235.7 20.9 %all_gather.18 = bf16[2,48,2048]{2,0,1:T(2,128)(2,1)S(1)} all-gather(bf16[2,3,2048]{2,0,1:T(2,128)(2,1)S(1)} %copy.23), channel_id=1, replica_groups=mesh['groups'=2,'blk'=16] {'blk'}, dimensions={1}, use_global_device_ids=true | all-gather | bytes 417792 | tf_op jit(solution)/shard_map/all_gather | solution.py:96
  256.6 8.4 %fusion.8 = bf16[4,2,48,2048]{3,2,0,1:T(8,128)(2,1)S(1)} fusion(bf16[2,48,768,1]{2,0,1,3:T(2,128)(2,1)S(1)} %bitcast.46, bf16[1,2,2048,768]{3,2,1,0:T(8,128)(2,1)S(1)} %fusion.5, bf16[1,2,2048,768]{3,2,1,0:T(8,128)(2,1)S(1)} %fusion.4, bf16[1,2,2048,768]{3,2,1,0:T(8,128)(2,1)S(1)} %fusion.3, bf16[1,2,2048,768]{3,2,1,0:T(8,128)(2,1)S(1)} %fusion.2), kind=kOutput, calls=%fused_computation.22 | convolution fusion | flops 1245708288 | bytes 26886144 | tf_op jit(solution)/shard_map/esf,kedf->kesd/dot_general | solution.py:99
  (113 shorter events, 42.0 us)
Async XLA Ops:
  6.5 16.5 %copy-start = (s32[128]{0:T(128)S(1)}, s32[128]{0:T(128)}, u32[]{:S(2)}) copy-start(s32[128]{0:T(128)} %param.14) | copy-start | bytes 1540
  6.5 139.0 %all-gather.6.cloned.1.call-start = ((), (), s32[]{:S(2)}) async-start(), calls=%async_computation.1 | async-start | bytes 2506752 | tf_op jit(solution)/shard_map/all_gather | solution.py:78
  7.3 202.6 %all-gather.4.cloned.1.call-start = ((), (), s32[]{:S(2)}) async-start(), calls=%async_computation | async-start | bytes 17825792 | tf_op jit(solution)/shard_map/all_gather | solution.py:77
  8.0 16.6 %collective-permute-start = (bf16[2,128,768]{2,1,0:T(8,128)(2,1)}, bf16[2,128,768]{2,1,0:T(8,128)(2,1)S(1)}, u32[]{:S(2)}, u32[]{:S(2)}) collective-permute-start(bf16[2,128,768]{2,1,0:T(8,128)(2,1)} %param.21), channel_id=1, source_target_pairs={{0,1},{1,2},{2,3},{3,4},{4,5},{5,6},{6,7},{7,8},{8,9},{9,10},{10,1... | collective-permute-start | bytes 1179656 | tf_op jit(solution)/shard_map/ppermute | solution.py:22
  8.5 16.2 %collective-permute-start.1 = (bf16[2,128,768]{2,1,0:T(8,128)(2,1)}, bf16[2,128,768]{2,1,0:T(8,128)(2,1)S(1)}, u32[]{:S(2)}, u32[]{:S(2)}) collective-permute-start(bf16[2,128,768]{2,1,0:T(8,128)(2,1)} %param.21), channel_id=1, source_target_pairs={{0,15},{1,0},{2,1},{3,2},{4,3},{5,4},{6,5},{7,6},{8,7},{9,8},{10,9... | collective-permute-start | bytes 1179656 | tf_op jit(solution)/shard_map/ppermute | solution.py:27
  24.6 11.5 %copy-start.2 = (bf16[2,128,768]{2,1,0:T(8,128)(2,1)}, bf16[2,128,768]{2,1,0:T(8,128)(2,1)S(1)}, u32[]{:S(2)}) copy-start(bf16[2,128,768]{2,1,0:T(8,128)(2,1)S(1)} %collective-permute-done) | copy-start | bytes 1179652
  24.6 11.4 %collective-permute-start.2 = (bf16[2,128,768]{2,1,0:T(8,128)(2,1)S(1)}, bf16[2,128,768]{2,1,0:T(8,128)(2,1)S(1)}, u32[]{:S(2)}, u32[]{:S(2)}) collective-permute-start(bf16[2,128,768]{2,1,0:T(8,128)(2,1)S(1)} %collective-permute-done), channel_id=1, source_target_pairs={{0,1},{1,2},{2,3},{3,4},{4,5},{5,6},{6,7},{7,8},{8,9},{9,10},{10,1... | collective-permute-start | bytes 1179656 | tf_op jit(solution)/shard_map/ppermute | solution.py:22
  24.7 11.3 %collective-permute-start.3 = (bf16[2,128,768]{2,1,0:T(8,128)(2,1)S(1)}, bf16[2,128,768]{2,1,0:T(8,128)(2,1)S(1)}, u32[]{:S(2)}, u32[]{:S(2)}) collective-permute-start(bf16[2,128,768]{2,1,0:T(8,128)(2,1)S(1)} %collective-permute-done.1), channel_id=1, source_target_pairs={{0,15},{1,0},{2,1},{3,2},{4,3},{5,4},{6,5},{7,6},{8,7},{9,8},{10,9... | collective-permute-start | bytes 1179656 | tf_op jit(solution)/shard_map/ppermute | solution.py:27
  36.0 15.5 %collective-permute-start.4 = (bf16[2,128,768]{2,1,0:T(8,128)(2,1)S(1)}, bf16[2,128,768]{2,1,0:T(8,128)(2,1)S(1)}, u32[]{:S(2)}, u32[]{:S(2)}) collective-permute-start(bf16[2,128,768]{2,1,0:T(8,128)(2,1)S(1)} %collective-permute-done.2), channel_id=1, source_target_pairs={{0,1},{1,2},{2,3},{3,4},{4,5},{5,6},{6,7},{7,8},{8,9},{9,10},{10,1... | collective-permute-start | bytes 1179656 | tf_op jit(solution)/shard_map/ppermute | solution.py:22
  36.1 28.9 %copy-start.4 = (bf16[2,128,768]{2,1,0:T(8,128)(2,1)}, bf16[2,128,768]{2,1,0:T(8,128)(2,1)S(1)}, u32[]{:S(2)}) copy-start(bf16[2,128,768]{2,1,0:T(8,128)(2,1)S(1)} %collective-permute-done.3) | copy-start | bytes 1179652
  36.1 16.7 %collective-permute-start.5 = (bf16[2,128,768]{2,1,0:T(8,128)(2,1)S(1)}, bf16[2,128,768]{2,1,0:T(8,128)(2,1)}, u32[]{:S(2)}, u32[]{:S(2)}) collective-permute-start(bf16[2,128,768]{2,1,0:T(8,128)(2,1)S(1)} %collective-permute-done.3), channel_id=1, source_target_pairs={{0,15},{1,0},{2,1},{3,2},{4,3},{5,4},{6,5},{7,6},{8,7},{9,8},{10,9... | collective-permute-start | bytes 1179656 | tf_op jit(solution)/shard_map/ppermute | solution.py:27
  51.5 13.5 %copy-start.6 = (bf16[2,128,768]{2,1,0:T(8,128)(2,1)}, bf16[2,128,768]{2,1,0:T(8,128)(2,1)S(1)}, u32[]{:S(2)}) copy-start(bf16[2,128,768]{2,1,0:T(8,128)(2,1)S(1)} %collective-permute-done.4) | copy-start | bytes 1179652
  51.5 13.2 %collective-permute-start.6 = (bf16[2,128,768]{2,1,0:T(8,128)(2,1)S(1)}, bf16[2,128,768]{2,1,0:T(8,128)(2,1)}, u32[]{:S(2)}, u32[]{:S(2)}) collective-permute-start(bf16[2,128,768]{2,1,0:T(8,128)(2,1)S(1)} %collective-permute-done.4), channel_id=1, source_target_pairs={{0,1},{1,2},{2,3},{3,4},{4,5},{5,6},{6,7},{7,8},{8,9},{9,10},{10,1... | collective-permute-start | bytes 1179656 | tf_op jit(solution)/shard_map/ppermute | solution.py:22
  52.8 38.0 %collective-permute-start.7 = (bf16[2,128,768]{2,1,0:T(8,128)(2,1)}, bf16[2,128,768]{2,1,0:T(8,128)(2,1)}, u32[]{:S(2)}, u32[]{:S(2)}) collective-permute-start(bf16[2,128,768]{2,1,0:T(8,128)(2,1)} %collective-permute-done.5), channel_id=1, source_target_pairs={{0,15},{1,0},{2,1},{3,2},{4,3},{5,4},{6,5},{7,6},{8,7},{9,8},{10,9... | collective-permute-start | bytes 1179656 | tf_op jit(solution)/shard_map/ppermute | solution.py:27
  64.7 28.0 %collective-permute-start.8 = (bf16[2,128,768]{2,1,0:T(8,128)(2,1)}, bf16[2,128,768]{2,1,0:T(8,128)(2,1)}, u32[]{:S(2)}, u32[]{:S(2)}) collective-permute-start(bf16[2,128,768]{2,1,0:T(8,128)(2,1)} %collective-permute-done.6), channel_id=1, source_target_pairs={{0,1},{1,2},{2,3},{3,4},{4,5},{5,6},{6,7},{7,8},{8,9},{9,10},{10,1... | collective-permute-start | bytes 1179656 | tf_op jit(solution)/shard_map/ppermute | solution.py:22
  66.1 23.1 %copy-start.1 = (bf16[2,128,768]{2,1,0:T(8,128)(2,1)S(1)}, bf16[2,128,768]{2,1,0:T(8,128)(2,1)}, u32[]{:S(2)}) copy-start(bf16[2,128,768]{2,1,0:T(8,128)(2,1)} %param.21) | copy-start | bytes 1179652
  66.3 23.6 %copy-start.3 = (bf16[2,128,768]{2,1,0:T(8,128)(2,1)S(1)}, bf16[2,128,768]{2,1,0:T(8,128)(2,1)}, u32[]{:S(2)}) copy-start(bf16[2,128,768]{2,1,0:T(8,128)(2,1)} %copy-done.2) | copy-start | bytes 1179652
  66.3 27.1 %copy-start.5 = (bf16[2,128,768]{2,1,0:T(8,128)(2,1)S(1)}, bf16[2,128,768]{2,1,0:T(8,128)(2,1)}, u32[]{:S(2)}) copy-start(bf16[2,128,768]{2,1,0:T(8,128)(2,1)} %copy-done.4) | copy-start | bytes 1179652
  90.8 15.1 %collective-permute-start.9 = (bf16[2,128,768]{2,1,0:T(8,128)(2,1)}, bf16[2,128,768]{2,1,0:T(8,128)(2,1)S(1)}, u32[]{:S(2)}, u32[]{:S(2)}) collective-permute-start(bf16[2,128,768]{2,1,0:T(8,128)(2,1)} %collective-permute-done.7), channel_id=1, source_target_pairs={{0,15},{1,0},{2,1},{3,2},{4,3},{5,4},{6,5},{7,6},{8,7},{9,8},{10,9... | collective-permute-start | bytes 1179656 | tf_op jit(solution)/shard_map/ppermute | solution.py:27
  92.7 19.5 %collective-permute-start.10 = (bf16[2,128,768]{2,1,0:T(8,128)(2,1)}, bf16[2,128,768]{2,1,0:T(8,128)(2,1)S(1)}, u32[]{:S(2)}, u32[]{:S(2)}) collective-permute-start(bf16[2,128,768]{2,1,0:T(8,128)(2,1)} %collective-permute-done.8), channel_id=1, source_target_pairs={{0,1},{1,2},{2,3},{3,4},{4,5},{5,6},{6,7},{7,8},{8,9},{9,10},{10,1... | collective-permute-start | bytes 1179656 | tf_op jit(solution)/shard_map/ppermute | solution.py:22
  105.9 15.3 %collective-permute-start.11 = (bf16[2,128,768]{2,1,0:T(8,128)(2,1)S(1)}, bf16[2,128,768]{2,1,0:T(8,128)(2,1)S(1)}, u32[]{:S(2)}, u32[]{:S(2)}) collective-permute-start(bf16[2,128,768]{2,1,0:T(8,128)(2,1)S(1)} %collective-permute-done.9), channel_id=1, source_target_pairs={{0,15},{1,0},{2,1},{3,2},{4,3},{5,4},{6,5},{7,6},{8,7},{9,8},{10,9... | collective-permute-start | bytes 1179656 | tf_op jit(solution)/shard_map/ppermute | solution.py:27
  112.2 14.4 %collective-permute-start.12 = (bf16[2,128,768]{2,1,0:T(8,128)(2,1)S(1)}, bf16[2,128,768]{2,1,0:T(8,128)(2,1)S(1)}, u32[]{:S(2)}, u32[]{:S(2)}) collective-permute-start(bf16[2,128,768]{2,1,0:T(8,128)(2,1)S(1)} %collective-permute-done.10), channel_id=1, source_target_pairs={{0,1},{1,2},{2,3},{3,4},{4,5},{5,6},{6,7},{7,8},{8,9},{9,10},{10,1... | collective-permute-start | bytes 1179656 | tf_op jit(solution)/shard_map/ppermute | solution.py:22
  121.2 18.1 %collective-permute-start.13 = (bf16[2,128,768]{2,1,0:T(8,128)(2,1)S(1)}, bf16[2,128,768]{2,1,0:T(8,128)(2,1)S(1)}, u32[]{:S(2)}, u32[]{:S(2)}) collective-permute-start(bf16[2,128,768]{2,1,0:T(8,128)(2,1)S(1)} %collective-permute-done.11), channel_id=1, source_target_pairs={{0,15},{1,0},{2,1},{3,2},{4,3},{5,4},{6,5},{7,6},{8,7},{9,8},{10,9... | collective-permute-start | bytes 1179656 | tf_op jit(solution)/shard_map/ppermute | solution.py:27
  126.6 18.1 %collective-permute-start.14 = (bf16[2,128,768]{2,1,0:T(8,128)(2,1)S(1)}, bf16[2,128,768]{2,1,0:T(8,128)(2,1)S(1)}, u32[]{:S(2)}, u32[]{:S(2)}) collective-permute-start(bf16[2,128,768]{2,1,0:T(8,128)(2,1)S(1)} %collective-permute-done.12), channel_id=1, source_target_pairs={{0,1},{1,2},{2,3},{3,4},{4,5},{5,6},{6,7},{7,8},{8,9},{9,10},{10,1... | collective-permute-start | bytes 1179656 | tf_op jit(solution)/shard_map/ppermute | solution.py:22
  (1 other events, 8.1 us)
Sparse Core Ops, SparseCore 0:
  9.6 53.8 all-gather.5
  65.7 144.1 all-gather.3
